TPU v7x, 512 devices: a whole 4x4x16 slice. The times are simulated.
512 devices in a mesh: mem: 64 (over x, y, z_hi, core), tile: 8 (over z_lo).
Axes of the slice: x: 4, y: 4, z: 16 (z_hi: 2, z_lo: 8; z = z_hi * 8 + z_lo), core: 2. Of those that a mesh axis runs over, the one named last changes fastest.
Arguments:
- members: float32 [64, 6, 512, 768], P('mem', None, 'tile'), may hold values from -6 to 6
- control: float32 [6, 512, 768], P(None, 'tile', 'mem'), may hold values from -6 to 6
- air_temp: float32 [512, 768], P('tile'), may hold values from -6 to 6
- flow_codes: int32 [512, 768], P('tile'), may hold values from 0 to 7
- ocean_mask: int32 [512, 768], P('tile'), may hold values 0 or 1
Outputs:
- advanced: float32 [64, 6, 512, 768], P('mem', None, 'tile')
All inputs are finite; a program needn't handle non-finite values. No bound on the sum of `ocean_mask` on one device may be relied on, other than what follows from the above.
Results may differ from a plain program's by a relative error of at most 0.00002.
Values sent between devices are 32-bit elements; how exact they have to be, the bound alone decides.
A program may use at most 64 MiB of HBM per device.

v0:
```python
import jax
import jax.numpy as jnp
from jax import lax
from jax.sharding import PartitionSpec as P

SUBSTEPS = 2


step_length = 0.5
drain_rate = 0.35
DIRECTIONS = ((0, 1), (1, 1), (1, 0), (1, -1), (0, -1), (-1, -1), (-1, 0), (-1, 1))


def with_halo(array, sides, width):
    for axis, dim in sides:
        size, length = (lax.axis_size(axis), array.shape[dim])
        up = [(i, (i + 1) % size) for i in range(size - 1)]
        down = [(j, i) for i, j in up]
        last = lax.slice_in_dim(array, length - width, length, axis=dim)
        first = lax.slice_in_dim(array, 0, width, axis=dim)
        before = lax.ppermute(last, axis, up)
        after = lax.ppermute(first, axis, down)
        array = jnp.concatenate([before, array, after], axis=dim)
    return array


def thermo(fields, air_temp, wet_mask):
    ice_cover, ice_thick, snow_depth = (fields[0], fields[1], fields[2])
    skin_temp, pond_depth, ocean_temp = (fields[3], fields[4], fields[5])
    insulation = jax.nn.softplus(ice_thick) + 0.5 * jax.nn.softplus(snow_depth) + 0.2
    conduction = (ocean_temp - skin_temp) / insulation
    melting = jax.nn.softplus(skin_temp)
    fraction = jax.nn.sigmoid(ice_cover)
    tendency = wet_mask * step_length
    new_cover = ice_cover + tendency * (conduction - melting)
    new_thick = ice_thick + tendency * (0.5 * conduction - melting * fraction)
    new_snow = snow_depth + tendency * (0.3 * jax.nn.sigmoid(-air_temp) - 0.5 * melting)
    new_skin = skin_temp + tendency * (air_temp - skin_temp + 0.1 * conduction)
    new_ocean = ocean_temp + tendency * (
        0.2 * (air_temp - ocean_temp) - 0.1 * conduction * fraction
    )
    new_pond = pond_depth + tendency * (0.5 * melting * fraction)
    stacked = jnp.stack([new_cover, new_thick, new_snow, new_skin, new_pond, new_ocean])
    return (stacked, wet_mask * drain_rate * new_pond)


def inflow(out_wide, code_wide):
    row_count = out_wide.shape[0] - 2
    col_count = out_wide.shape[1]
    out_pad = jnp.pad(out_wide, ((0, 0), (1, 1)))
    code_pad = jnp.pad(code_wide, ((0, 0), (1, 1)), constant_values=-1)
    arrived = jnp.zeros((row_count, col_count), out_wide.dtype)
    for number, (row_step, col_step) in enumerate(DIRECTIONS):
        source = out_pad[
            1 - row_step : 1 - row_step + row_count, 1 - col_step : 1 - col_step + col_count
        ]
        matches = (
            code_pad[
                1 - row_step : 1 - row_step + row_count, 1 - col_step : 1 - col_step + col_count
            ]
            == number
        )
        arrived = arrived + jnp.where(matches, source, 0.0)
    return arrived


def shards(members, control, air_temp, flow_codes, ocean_mask):
    own_state = members[0]
    member_total = lax.axis_size("mem")
    ensemble_mean = lax.psum(own_state, "mem") / member_total
    full_control = lax.all_gather(control, "mem", axis=2, tiled=True)
    start_state = own_state - ensemble_mean + full_control
    wet_mask = ocean_mask.astype(jnp.float32)
    code_wide = with_halo(flow_codes, (("tile", 0),), 1)
    fields = start_state
    for substep in range(SUBSTEPS):
        stacked, outflow = thermo(fields, air_temp, wet_mask)
        out_wide = with_halo(outflow, (("tile", 0),), 1)
        new_pond = stacked[4] - outflow + wet_mask * inflow(out_wide, code_wide)
        fields = stacked.at[4].set(new_pond)
    return fields[None]


def solution(mesh):
    in_specs = (
        P("mem", None, "tile", None),
        P(None, "tile", "mem"),
        P("tile", None),
        P("tile", None),
        P("tile", None),
    )
    out_specs = P("mem", None, "tile", None)
    return jax.shard_map(shards, mesh=mesh, in_specs=in_specs, out_specs=out_specs, check_vma=False)
```

profile of v0, /device:TPU:1, one launch (start us, length us, event | category | flops | bytes accessed | tf_op | source)
XLA Modules:
  0.0 1213.8 jit_solution(17123060915428200607)
XLA Ops:
  6.5 0.0 copy-start.3
  6.5 0.0 all-gather.2.cloned.1.call-start
  6.5 1.5 copy.26
  8.0 0.0 all-gather.2.cloned.1.call-update
  8.0 0.0 all-reduce.5.cloned.1.call-start
  8.1 0.7 all-reduce.5.cloned.1.call-update
  8.8 0.0 copy-done.3
  8.8 1.3 collective-permute-start.1
  10.1 0.0 copy-start.2
  10.1 5.1 collective-permute-start
  15.3 124.5 %all-gather.2.cloned.1.call-done = f32[6,64,768]{1,0,2:T(8,128)} async-done(((f32[6,64,12]{1,0,2:T(8,128)}), f32[6,64,768]{1,0,2:T(8,128)}) %all-gather.2.cloned.1.call-update) | async-done | bytes 1179664 | tf_op jit(solution)/shard_map/all_gather | solution.py:71
  139.7 2.3 copy.27
  142.0 0.0 copy-start
  142.0 1046.6 %all-reduce.5.cloned.1.call-done = f32[6,64,768]{2,1,0:T(8,128)} async-done(((f32[6,64,768]{2,1,0:T(8,128)}), f32[6,64,768]{2,1,0:T(8,128)}) %all-reduce.5.cloned.1.call-update) | async-done | bytes 1179664 | tf_op jit(solution)/shard_map/psum | solution.py:70
  1188.6 0.0 copy-done.2
  1188.6 1.5 subtract_add_fusion
  1190.0 0.0 copy-done
  1190.0 0.0 copy-start.1
  1190.1 0.2 fusion.44
  1190.3 1.3 collective-permute-start.3
  1191.6 4.0 collective-permute-start.2
  1195.6 0.0 collective-permute-done.1
  1195.6 0.0 collective-permute-done
  1195.6 0.0 collective-permute-done.3
  1195.6 0.7 collective-permute-done.2
  1196.3 0.1 select_maximum_fusion.2
  1196.4 0.0 copy-done.1
  1196.5 1.3 fusion.43
  1197.8 0.7 bitcast_dynamic-update-slice_fusion.5
  1198.4 0.3 bitcast_dynamic-update-slice_fusion.4
  1198.8 0.3 bitcast_dynamic-update-slice_fusion.3
  1199.1 0.1 bitcast_dynamic-update-slice_fusion.2
  1199.2 1.3 collective-permute-start.5
  1200.5 4.2 collective-permute-start.4
  1204.7 0.2 bitcast_dynamic-update-slice_fusion
  1204.9 0.0 copy-start.4
  1204.9 0.0 collective-permute-done.5
  1204.9 0.5 collective-permute-done.4
  1205.4 0.1 select_maximum_fusion
  1205.6 0.3 copy-done.4
  1205.9 1.0 fusion.19
  (5 shorter events, 0.1 us)
Async XLA Ops:
  6.5 2.3 copy-start.3
  6.5 133.2 %all-gather.2.cloned.1.call-start = ((), (), s32[]{:S(2)}) async-start(), calls=%async_computation.1 | async-start | bytes 3194880 | tf_op jit(solution)/shard_map/all_gather | solution.py:71
  8.0 1180.5 %all-reduce.5.cloned.1.call-start = ((), (), s32[]{:S(2)}) async-start(), calls=%async_computation | async-start | bytes 2359296 | tf_op jit(solution)/shard_map/psum | solution.py:70
  8.8 1186.8 %collective-permute-start.1 = (s32[1,768]{1,0:T(1,128)S(1)}, s32[1,768]{1,0:T(1,128)S(1)}, u32[]{:S(2)}, u32[]{:S(2)}) collective-permute-start(s32[1,768]{1,0:T(1,128)S(1)} %get-tuple-element.47), channel_id=1, source_target_pairs={{1,0},{2,1},{3,2},{4,3},{5,4},{6,5},{7,6},{9,8},{10,9},{11,10},{12... | collective-permute-start | bytes 9224 | tf_op jit(solution)/shard_map/ppermute | solution.py:22
  10.1 1178.4 %copy-start.2 = (f32[1,6,64,768]{3,2,1,0:T(8,128)S(1)}, f32[1,6,64,768]{3,2,1,0:T(8,128)}, u32[]{:S(2)}) copy-start(f32[1,6,64,768]{3,2,1,0:T(8,128)} %param.9) | copy-start | bytes 3538948
  10.1 1185.5 %collective-permute-start = (s32[1,768]{1,0:T(1,128)S(1)}, s32[1,768]{1,0:T(1,128)S(1)}, u32[]{:S(2)}, u32[]{:S(2)}) collective-permute-start(s32[1,768]{1,0:T(1,128)S(1)} %get-tuple-element.46), channel_id=1, source_target_pairs={{0,1},{1,2},{2,3},{3,4},{4,5},{5,6},{6,7},{8,9},{9,10},{10,11},{11... | collective-permute-start | bytes 9224 | tf_op jit(solution)/shard_map/ppermute | solution.py:21
  142.0 1048.1 %copy-start = (s32[64,768]{1,0:T(8,128)S(1)}, s32[64,768]{1,0:T(8,128)}, u32[]{:S(2)}) copy-start(s32[64,768]{1,0:T(8,128)} %param.13) | copy-start | bytes 589828
  1190.0 6.4 copy-start.1
  1190.3 5.3 collective-permute-start.3
  1191.6 4.7 collective-permute-start.2
  1199.2 5.8 collective-permute-start.5
  1200.5 5.0 collective-permute-start.4
  1204.9 1.0 copy-start.4
Sparse Core Ops, SparseCore 0:
  11.7 127.9 all-gather.1
  142.6 1045.8 all-reduce.4
where the time goes:
time: 1220 us; the launch traced here: 1210 us
  waiting for transfers between devices  1170 us (96%)
  starting transfers between devices  17.3 us (1%)
  between operations  13.6 us (1%)
    psum x1, waiting for transfers between devices, shards(): ensemble_mean = lax.psum(own_state, 'mem') / member_total  1050 us
    all_gather x1, waiting for transfers between devices, shards(): full_control = lax.all_gather(control, 'mem', axis=2, tiled=True)  124 us
  transfers between devices with their start and end apart: 8, of which 4 were waited for; matrix products, arithmetic and copies ran while one was open for 0% of the time, Pallas kernels for 0%

commit v1 on v0

v1 whole, which is shorter than its diff:
```python
import functools

import jax
import jax.numpy as jnp
from jax import lax
from jax.experimental import pallas as pl
from jax.experimental.pallas import tpu as pltpu
from jax.sharding import PartitionSpec as P

MESH = pl.DeviceIdType.MESH
SUBSTEPS = 2
MEMBERS = 64
DIRECTIONS = ((0, 1), (1, 1), (1, 0), (1, -1), (0, -1), (-1, -1), (-1, 0), (-1, 1))
STEPS = sorted(
    ((dx, dy) for dx in range(4) for dy in range(4)),
    key=lambda s: -(min(s[0], 4 - s[0]) + min(s[1], 4 - s[1])),
)
PEERS = len(STEPS) - 1


def softplus(v):
    return jnp.maximum(v, 0.0) + jnp.log1p(jnp.exp(-jnp.abs(v)))


def sigmoid(v):
    return 1.0 / (1.0 + jnp.exp(-v))


def block(ref, half, part):
    columns = pl.ds(pl.multiple_of((part % 2) * 384, 128), 384)
    return ref.at[pl.ds(3 * half, 3), part // 2, :, columns]


def kernel(
    members, control, air_temp, flow_codes, ocean_mask, advanced,
    own, raw, shift, state, core_in, plane_in, depth_out, depth_in, strip, air, code, mask, gain, outflow,
    local_sem, core_send, core_recv, plane_send, plane_recv, depth_sem,
    gather_send, gather_recv, share_send, share_recv, edge_send, edge_recv,
):
    m, t = lax.axis_index("mem"), lax.axis_index("tile")
    x, y, z, c = m // 16, (m // 4) % 4, (m // 2) % 2, m % 2

    def device(x, y, z, c):
        return (((x * 4 + y) * 2 + z) * 2 + c, t)

    sibling = device(x, y, z, 1 - c)
    far = device(x, y, 1 - z, c)
    here = x * 4 + y
    to = [((x + dx) % 4, (y + dy) % 4) for dx, dy in STEPS]
    come = [((x + 4 - dx) % 4, (y + 4 - dy) % 4) for dx, dy in STEPS]
    goal = [a * 4 + b for a, b in to]
    origin = [a * 4 + b for a, b in come]
    above, below = (m, jnp.maximum(t - 1, 0)), (m, jnp.minimum(t + 1, 7))
    has_above, has_below = t > 0, t < 7

    loads = [
        pltpu.make_async_copy(s, d, local_sem.at[i])
        for i, (s, d) in enumerate((
            (members, own), (control, strip), (air_temp, air), (ocean_mask, mask),
            (flow_codes, code.at[pl.ds(1, 8)]), (members, raw),
        ))
    ]
    for copy in loads:
        copy.start()

    barrier = pltpu.get_barrier_semaphore()
    for target in [sibling, far] + [device(a, b, z, c) for a, b in to[:PEERS]]:
        pl.semaphore_signal(barrier, inc=1, device_id=target, device_id_type=MESH)

    @pl.when(has_above)
    def _():
        pl.semaphore_signal(barrier, inc=1, device_id=above, device_id_type=MESH)

    @pl.when(has_below)
    def _():
        pl.semaphore_signal(barrier, inc=1, device_id=below, device_id_type=MESH)

    loads[0].wait()
    loads[1].wait()
    tile_at = jnp.minimum((12 * m) // 128, 4)
    span = pl.ds(pl.multiple_of(tile_at * 128, 128), 256)
    turn = 12 * m - 128 * tile_at

    def place(r, carry):
        piece = jnp.pad(strip[r // 8, r % 8], ((0, 0), (0, 244)))
        piece = pltpu.roll(piece, turn, 1)
        own[r // 8, r % 8, :, span] = own[r // 8, r % 8, :, span] - float(MEMBERS) * piece
        return carry

    lax.fori_loop(0, 48, place, 0)
    for i in (2, 3, 4, 5):
        loads[i].wait()
    for r in range(8):
        gain[r] = 0.3 * sigmoid(-air[r])

    for edge, missing in ((0, t == 0), (9, t == 7)):
        @pl.when(missing)
        def _():
            code[edge] = jnp.full((8, 768), -1, jnp.int32)
            for s in range(SUBSTEPS):
                outflow[s, edge] = jnp.zeros((8, 768), jnp.float32)

    extra = jnp.where(has_above, 1, 0) + jnp.where(has_below, 1, 0)
    pl.semaphore_wait(barrier, PEERS + 2 + extra)

    def remote(src, dst, send, recv, target):
        return pltpu.make_async_remote_copy(
            src_ref=src, dst_ref=dst, send_sem=send, recv_sem=recv, device_id=target, device_id_type=MESH)

    def edges(buffer, slot):
        up = remote(buffer.at[1], buffer.at[9], edge_send.at[slot, 0], edge_recv.at[slot, 0], above)
        down = remote(buffer.at[8], buffer.at[0], edge_send.at[slot, 1], edge_recv.at[slot, 1], below)
        return up, down

    def start_edges(buffer, slot):
        up, down = edges(buffer, slot)
        pl.when(has_above)(up.start)
        pl.when(has_below)(down.start)

    def wait_edges(buffer, slot):
        up, down = edges(buffer, slot)

        @pl.when(has_above)
        def _():
            up.wait_send()
            down.wait_recv()

        @pl.when(has_below)
        def _():
            down.wait_send()
            up.wait_recv()

    core_copies = [
        remote(block(own, 1 - c, goal[j]), core_in.at[j], core_send.at[j], core_recv.at[j], sibling)
        for j in range(PEERS + 1)
    ]
    for copy in core_copies:
        copy.start()
    start_edges(code, 0)

    plane_copies = []
    for j in range(PEERS + 1):
        core_copies[j].wait_recv()
        core_in[j] = core_in[j] + block(own, c, goal[j])[...]
        if j < PEERS:
            copy = remote(
                core_in.at[j], plane_in.at[j], plane_send.at[j], plane_recv.at[j], device(*to[j], z, c))
            copy.start()
            plane_copies.append(copy)
    total = core_in[PEERS]
    for j in reversed(range(PEERS)):
        plane_copies[j].wait_recv()
        total = total + plane_in[j]
    depth_out[...] = total

    copy = remote(depth_out, depth_in, depth_sem.at[0], depth_sem.at[1], far)
    copy.start()
    copy.wait_recv()
    block(shift, c, here)[...] = (depth_out[...] + depth_in[...]) * (-1.0 / MEMBERS)
    copy.wait_send()

    gather_copies, share_copies = [], []
    for j in range(PEERS):
        mine = block(shift, c, here)
        copy = remote(mine, mine, gather_send.at[j], gather_recv.at[j], device(*to[j], z, c))
        copy.start()
        gather_copies.append(copy)
    for j in reversed(range(PEERS + 1)):
        part = block(shift, c, origin[j])
        if j < PEERS:
            arriving = remote(part, part, gather_send.at[j], gather_recv.at[j], sibling)
            arriving.wait_recv()
        copy = remote(part, part, share_send.at[j], share_recv.at[j], sibling)
        copy.start()
        share_copies.append(copy)
    for copy in core_copies + plane_copies + gather_copies + share_copies:
        copy.wait_send()
    for j in range(PEERS + 1):
        part = block(shift, 1 - c, origin[j])
        remote(part, part, share_send.at[j], share_recv.at[j], sibling).wait_recv()
    wait_edges(code, 0)

    column = lax.broadcasted_iota(jnp.int32, (8, 768), 1)
    for s in range(SUBSTEPS):
        def thermo(n, carry):
            r = n
            if s == 0:
                cover, thick, snow, skin, pond, ocean = [raw[f, r] + shift[f, r] for f in range(6)]
            else:
                cover, thick, snow, skin, pond, ocean = [state[f, r] for f in range(6)]
            wet = mask[r].astype(jnp.float32)
            warm = air[r]
            step = 0.5 * wet
            conduction = (ocean - skin) / (softplus(thick) + 0.5 * softplus(snow) + 0.2)
            melting = softplus(skin)
            fraction = sigmoid(cover)
            drained = melting * fraction
            state[0, r] = cover + step * (conduction - melting)
            state[1, r] = thick + step * (0.5 * conduction - drained)
            state[2, r] = snow + step * (gain[r] - 0.5 * melting)
            state[3, r] = skin + step * (warm - skin + 0.1 * conduction)
            state[5, r] = ocean + step * (0.2 * (warm - ocean) - 0.1 * conduction * fraction)
            pond = pond + step * (0.5 * drained)
            state[4, r] = pond
            outflow[s, r + 1] = 0.35 * wet * pond
            return carry

        thermo(0, 0)
        thermo(7, 0)
        start_edges(outflow.at[s], 1 + s)
        lax.fori_loop(1, 7, thermo, 0)
        if s == SUBSTEPS - 1:
            stores = [
                pltpu.make_async_copy(state.at[pl.ds(f, n)], advanced.at[pl.ds(f, n)], local_sem.at[i])
                for i, (f, n) in enumerate(((0, 4), (5, 1), (4, 1)))
            ]
            stores[0].start()
            stores[1].start()
        wait_edges(outflow.at[s], 1 + s)

        row = lax.broadcasted_iota(jnp.int32, (8, 768), 0)

        def drain(r, carry):
            flows = [outflow[s, r + d] for d in range(3)]
            codes = [code[r + d] for d in range(3)]

            def sent(number, d):
                return jnp.where(codes[d] == number, flows[d], 0.0)

            down = {dc: k for k, (dr, dc) in enumerate(DIRECTIONS) if dr == 1}
            up = {dc: k for k, (dr, dc) in enumerate(DIRECTIONS) if dr == -1}
            level = {dc: k for k, (dr, dc) in enumerate(DIRECTIONS) if dr == 0}
            sums = {}
            for dc in (-1, 0, 1):
                before = pltpu.roll(jnp.where(row == 7, sent(down[dc], 0), sent(down[dc], 1)), 1, 0)
                after = pltpu.roll(jnp.where(row == 0, sent(up[dc], 2), sent(up[dc], 1)), 7, 0)
                sums[dc] = before + after
                if dc:
                    sums[dc] = sums[dc] + sent(level[dc], 1)
            right = jnp.where(column == 0, 0.0, pltpu.roll(sums[1], 1, 1))
            left = jnp.where(column == 767, 0.0, pltpu.roll(sums[-1], 767, 1))
            arrived = sums[0] + right + left
            state[4, r] = state[4, r] - flows[1] + mask[r].astype(jnp.float32) * arrived
            return carry

        lax.fori_loop(0, 8, drain, 0)
    stores[2].start()
    for copy in stores:
        copy.wait()


def solution(mesh):
    hbm = pl.BlockSpec(memory_space=pltpu.MemorySpace.HBM)
    whole = (6, 8, 8, 768)
    f32, i32 = jnp.float32, jnp.int32
    dma = pltpu.SemaphoreType.DMA
    n = PEERS + 1

    def shards(members, control, air_temp, flow_codes, ocean_mask):
        rows = (8, 8, 768)
        result = pl.pallas_call(
            kernel,
            out_shape=jax.ShapeDtypeStruct(whole, f32),
            in_specs=[hbm] * 5,
            out_specs=hbm,
            scratch_shapes=[
                pltpu.VMEM(whole, f32), pltpu.VMEM(whole, f32), pltpu.VMEM(whole, f32), pltpu.VMEM(whole, f32),
                pltpu.VMEM((n, 3, 8, 384), f32), pltpu.VMEM((n - 1, 3, 8, 384), f32),
                pltpu.VMEM((3, 8, 384), f32), pltpu.VMEM((3, 8, 384), f32),
                pltpu.VMEM((6, 8, 8, 12), f32), pltpu.VMEM(rows, f32), pltpu.VMEM((10, 8, 768), i32),
                pltpu.VMEM(rows, i32), pltpu.VMEM(rows, f32), pltpu.VMEM((SUBSTEPS, 10, 8, 768), f32),
                dma((6,)), dma((n,)), dma((n,)), dma((n - 1,)), dma((n - 1,)), dma((2,)),
                dma((n - 1,)), dma((n - 1,)), dma((n,)), dma((n,)), dma((3, 2)), dma((3, 2)),
            ],
            compiler_params=pltpu.CompilerParams(
                collective_id=0, has_side_effects=True, vmem_limit_bytes=32 * 1024 * 1024),
            name="recentre_advance",
        )(
            members.reshape(whole), control.reshape(6, 8, 8, 12), air_temp.reshape(rows),
            flow_codes.reshape(rows), ocean_mask.reshape(rows),
        )
        return result.reshape(1, 6, 64, 768)

    tiles = P("tile", None)
    return jax.shard_map(
        shards, mesh=mesh,
        in_specs=(P("mem", None, "tile", None), P(None, "tile", "mem"), tiles, tiles, tiles),
        out_specs=P("mem", None, "tile", None), check_vma=False)
```

time: 1220 us -> 59.9 us (0.05)
  waiting for transfers between devices: 1170 us -> 0 us
  Pallas kernels: 0 us -> 53.7 us
  starting transfers between devices: 17.3 us -> 0 us
  between operations: 13.6 us -> 0.03 us
    psum x1 -> x0, waiting for transfers between devices: 1050 us -> none  [shards(): ensemble_mean = lax.psum(own_state, 'mem') / member_total]
    all_gather x1 -> x0, waiting for transfers between devices: 124 us -> none  [shards(): full_control = lax.all_gather(control, 'mem', axis=2, tiled=True)]
    pallas_call x0 -> x1, Pallas kernels: none -> 53.7 us  [shards(): pl.pallas_call(kernel, out_shape=jax.ShapeDtypeStruct(whole, f32), in_spe...]
    ppermute x6 -> x0, starting transfers between devices: 17.2 us -> none  [the longest x3 13.4 us: with_halo(): before = lax.ppermute(last, axis, up)]
  transfers between devices with their start and end apart: 8 -> 0, of which waited for: 4 -> 0; matrix products, arithmetic and copies ran while one was open for 0% -> 0% of each run, Pallas kernels for 0% -> 0%
where the time goes in v1:
time: 59.9 us; the launch traced here: 59.7 us
  Pallas kernels  53.7 us (90%)
  local copies, waits for them, and re-layouts  5.98 us (10%)
    pallas_call x1, Pallas kernels, shards(): pl.pallas_call(kernel, out_shape=jax.ShapeDtypeStruct(whole, f32), in_spe...  53.7 us
    unnamed x10, local copies, waits for them, and re-layouts  5.98 us

profile of v1, /device:TPU:1, one launch (start us, length us, event | category | flops | bytes accessed | tf_op | source)
XLA Modules:
  0.0 59.7 jit_solution(3239189791044400388)
XLA Ops:
  0.0 0.9 %copy.6 = f32[6,64,12]{2,1,0:T(8,128)S(1)} copy(f32[6,64,12]{1,2,0:T(8,128)} %param.6) | data formatting | bytes 36864 | tf_op args[1]
  0.9 0.0 copy-start
  0.9 1.3 %copy-done = f32[1,6,64,768]{3,2,1,0:T(8,128)S(1)} copy-done((f32[1,6,64,768]{3,2,1,0:T(8,128)S(1)}, f32[1,6,64,768]{3,2,1,0:T(8,128)}, u32[]{:S(2)}) %copy-start) | copy-done | bytes 1179672
  2.2 0.0 copy-start.1
  2.2 0.9 %copy-done.1 = f32[64,768]{1,0:T(8,128)S(1)} copy-done((f32[64,768]{1,0:T(8,128)S(1)}, f32[64,768]{1,0:T(8,128)}, u32[]{:S(2)}) %copy-start.1) | copy-done | bytes 196632
  3.1 0.0 copy-start.2
  3.1 0.9 %copy-done.2 = s32[64,768]{1,0:T(8,128)S(1)} copy-done((s32[64,768]{1,0:T(8,128)S(1)}, s32[64,768]{1,0:T(8,128)}, u32[]{:S(2)}) %copy-start.2) | copy-done | bytes 196632
  4.1 0.0 copy-start.3
  4.1 0.9 %copy-done.3 = s32[64,768]{1,0:T(8,128)S(1)} copy-done((s32[64,768]{1,0:T(8,128)S(1)}, s32[64,768]{1,0:T(8,128)}, u32[]{:S(2)}) %copy-start.3) | copy-done | bytes 196632
  5.0 53.7 %recentre_advance.1 = f32[6,8,8,768]{3,2,1,0:T(8,128)S(1)} custom-call(f32[6,8,8,768]{3,2,1,0:T(8,128)S(1)} %bitcast.7, f32[6,8,8,12]{3,2,1,0:T(8,128)S(1)} %bitcast.8, f32[8,8,768]{2,1,0:T(8,128)S(1)} %bitcast.9, s32[8,8,768]{2,1,0:T(8,128)S(1)} %bitcast.10, s32[8,8,768]{2,1,0:T(8,128)S(1)} %bitcast.11), custom_call_target="tpu_custom_call" | custom-call | tf_op jit(solution)/shard_map/recentre_advance/pallas_call | solution.py:261
  58.6 1.0 %copy.8 = f32[1,6,64,768]{3,2,1,0:T(8,128)} copy(f32[1,6,64,768]{3,2,1,0:T(8,128)S(1)} %bitcast.6) | data formatting | bytes 2359296
Async XLA Ops:
  0.9 1.3 %copy-start = (f32[1,6,64,768]{3,2,1,0:T(8,128)S(1)}, f32[1,6,64,768]{3,2,1,0:T(8,128)}, u32[]{:S(2)}) copy-start(f32[1,6,64,768]{3,2,1,0:T(8,128)} %param.5) | copy-start | bytes 3538948
  2.2 0.9 %copy-start.1 = (f32[64,768]{1,0:T(8,128)S(1)}, f32[64,768]{1,0:T(8,128)}, u32[]{:S(2)}) copy-start(f32[64,768]{1,0:T(8,128)} %param.7) | copy-start | bytes 589828
  3.1 0.9 %copy-start.2 = (s32[64,768]{1,0:T(8,128)S(1)}, s32[64,768]{1,0:T(8,128)}, u32[]{:S(2)}) copy-start(s32[64,768]{1,0:T(8,128)} %param.8) | copy-start | bytes 589828
  4.1 0.9 %copy-start.3 = (s32[64,768]{1,0:T(8,128)S(1)}, s32[64,768]{1,0:T(8,128)}, u32[]{:S(2)}) copy-start(s32[64,768]{1,0:T(8,128)} %param.9) | copy-start | bytes 589828

commit v2 on v1

v2 whole, which is shorter than its diff:
```python
import jax
import jax.numpy as jnp
from jax import lax
from jax.experimental import pallas as pl
from jax.experimental.pallas import tpu as pltpu
from jax.sharding import PartitionSpec as P

MESH = pl.DeviceIdType.MESH
SUBSTEPS = 2
VMEM_LIMIT = 60 * 1024 * 1024
MEMBERS = 64
DIRECTIONS = ((0, 1), (1, 1), (1, 0), (1, -1), (0, -1), (-1, -1), (-1, 0), (-1, 1))
STEPS = sorted(
    ((dx, dy) for dx in range(4) for dy in range(4)),
    key=lambda s: -(min(s[0], 4 - s[0]) + min(s[1], 4 - s[1])),
)
PEERS = len(STEPS) - 1


def softplus(v):
    return jnp.maximum(v, 0.0) + jnp.log1p(jnp.exp(-jnp.abs(v)))


def sigmoid(v):
    return 1.0 / (1.0 + jnp.exp(-v))


def block(field, part):
    columns = pl.ds(pl.multiple_of((part % 2) * 384, 128), 384)
    return field.at[part // 2, :, columns]


def of_core(i, c):
    return (3 * c, 4 - 3 * c, 5 - 3 * c)[i]


def kernel(
    members, control, air_temp, flow_codes, ocean_mask, state,
    own, raw, shift, core_in, plane_in, depth_out, depth_in, strip, air, code, mask, gain, keep, outflow,
    local_sem, core_send, core_recv, plane_send, plane_recv, depth_send, depth_recv,
    gather_send, gather_recv, share_send, share_recv, edge_send, edge_recv,
):
    m, t = lax.axis_index("mem"), lax.axis_index("tile")
    x, y, z, c = m // 16, (m // 4) % 4, (m // 2) % 2, m % 2

    def device(x, y, z, c):
        return (((x * 4 + y) * 2 + z) * 2 + c, t)

    sibling = device(x, y, z, 1 - c)
    far = device(x, y, 1 - z, c)
    here = x * 4 + y
    to = [((x + dx) % 4, (y + dy) % 4) for dx, dy in STEPS]
    come = [((x + 4 - dx) % 4, (y + 4 - dy) % 4) for dx, dy in STEPS]
    goal = [a * 4 + b for a, b in to]
    origin = [a * 4 + b for a, b in come]
    above, below = (m, jnp.maximum(t - 1, 0)), (m, jnp.minimum(t + 1, 7))
    has_above, has_below = t > 0, t < 7

    loads = [
        pltpu.make_async_copy(s, d, local_sem.at[i])
        for i, (s, d) in enumerate((
            (members, own), (control, strip), (air_temp, air), (ocean_mask, mask),
            (flow_codes, code.at[pl.ds(1, 8)]), (members, raw),
        ))
    ]
    for copy in loads:
        copy.start()

    barrier = pltpu.get_barrier_semaphore()
    for target in [sibling, far] + [device(a, b, z, c) for a, b in to[:PEERS]]:
        pl.semaphore_signal(barrier, inc=1, device_id=target, device_id_type=MESH)

    @pl.when(has_above)
    def _():
        pl.semaphore_signal(barrier, inc=1, device_id=above, device_id_type=MESH)

    @pl.when(has_below)
    def _():
        pl.semaphore_signal(barrier, inc=1, device_id=below, device_id_type=MESH)

    loads[0].wait()
    loads[1].wait()
    tile_at = jnp.minimum((12 * m) // 128, 4)
    span = pl.ds(pl.multiple_of(tile_at * 128, 128), 256)
    lane = lax.broadcasted_iota(jnp.int32, (12, 256), 1) + 128 * tile_at - 12 * m
    spread = jnp.where(lane == lax.broadcasted_iota(jnp.int32, (12, 256), 0), -float(MEMBERS), 0.0)
    for f in range(6):
        placed = lax.dot_general(
            strip[f], spread, (((0,), (0,)), ((), ())),
            precision=lax.Precision.HIGHEST, preferred_element_type=jnp.float32)
        for r in range(8):
            own[f, r, :, span] = own[f, r, :, span] + placed[8 * r:8 * r + 8]
    for i in (2, 3, 4, 5):
        loads[i].wait()
    for r in range(8):
        gain[r] = 0.3 * sigmoid(-air[r])

    for edge, missing in ((0, t == 0), (9, t == 7)):
        @pl.when(missing)
        def _():
            code[edge] = jnp.full((8, 768), -1, jnp.int32)
            for s in range(SUBSTEPS):
                outflow[s, edge] = jnp.zeros((8, 768), jnp.float32)

    extra = jnp.where(has_above, 1, 0) + jnp.where(has_below, 1, 0)
    pl.semaphore_wait(barrier, PEERS + 2 + extra)

    def remote(src, dst, send, recv, target):
        return pltpu.make_async_remote_copy(
            src_ref=src, dst_ref=dst, send_sem=send, recv_sem=recv, device_id=target, device_id_type=MESH)

    def edges(buffer, slot):
        up = remote(buffer.at[1], buffer.at[9], edge_send.at[slot, 0], edge_recv.at[slot, 0], above)
        down = remote(buffer.at[8], buffer.at[0], edge_send.at[slot, 1], edge_recv.at[slot, 1], below)
        return up, down

    def start_edges(buffer, slot):
        up, down = edges(buffer, slot)
        pl.when(has_above)(up.start)
        pl.when(has_below)(down.start)

    def wait_edges(buffer, slot):
        up, down = edges(buffer, slot)

        @pl.when(has_above)
        def _():
            up.wait_send()
            down.wait_recv()

        @pl.when(has_below)
        def _():
            down.wait_send()
            up.wait_recv()

    rounds = range(3)
    pack = plane_in.at[0]

    core_copies = [
        remote(own.at[of_core(i, 1 - c)], core_in.at[i], core_send.at[i], core_recv.at[i], sibling)
        for i in rounds
    ]
    for copy in core_copies:
        copy.start()
    start_edges(code, 0)

    for i in rounds:
        core_copies[i].wait_recv()
        for j in range(PEERS + 1):
            mine = block(core_in.at[i], goal[j])
            mine[...] = mine[...] + block(own.at[of_core(i, c)], goal[j])[...]
            if j < PEERS:
                remote(mine, plane_in.at[i, j], plane_send.at[i], plane_recv.at[i], device(*to[j], z, c)).start()

    depth_copies = [
        remote(depth_out.at[i], depth_in.at[i], depth_send.at[i], depth_recv.at[i], far) for i in rounds
    ]
    for i in rounds:
        remote(pack, pack, plane_send.at[i], plane_recv.at[i], sibling).wait_recv()
        total = block(core_in.at[i], here)[...]
        for j in range(PEERS):
            total = total + plane_in[i, j]
        depth_out[i] = total
        depth_copies[i].start()

    for i in rounds:
        depth_copies[i].wait_recv()
        mine = block(shift.at[of_core(i, c)], here)
        mine[...] = (depth_out[i] + depth_in[i]) * (-1.0 / MEMBERS)
        for j in range(PEERS):
            remote(mine, mine, gather_send.at[i], gather_recv.at[i], device(*to[j], z, c)).start()

    def share(i, c):
        field = shift.at[of_core(i, c)]
        return remote(field, field, share_send.at[i], share_recv.at[i], sibling)

    def pass_on(i):
        remote(pack, pack, gather_send.at[i], gather_recv.at[i], sibling).wait_recv()
        share(i, c).start()

    def field(f, r):
        return raw[f, r] + shift[f, r]

    def wet(r):
        return mask[r].astype(jnp.float32)

    def melt(r, carry=0):
        cover, skin = field(0, r), field(3, r)
        step = 0.5 * wet(r)
        melting = softplus(skin)
        fraction = sigmoid(cover)
        keep[0, r] = step * (melting * fraction)
        keep[1, r] = skin
        keep[2, r] = fraction
        state[0, r] = cover - step * melting
        state[2, r] = step * (gain[r] - 0.5 * melting)
        state[3, r] = skin + step * (air[r] - skin)
        return carry

    def pool(r, carry=0):
        drained = keep[0, r]
        pond = field(4, r) + 0.5 * drained
        state[4, r] = pond
        outflow[0, r + 1] = 0.35 * wet(r) * pond
        thick = field(1, r)
        state[1, r] = thick - drained
        keep[0, r] = softplus(thick) + 0.2
        return carry

    def conduct(r, carry=0):
        ocean, snow = field(5, r), field(2, r)
        step = 0.5 * wet(r)
        flux = step * ((ocean - keep[1, r]) / (keep[0, r] + 0.5 * softplus(snow)))
        state[0, r] = state[0, r] + flux
        state[1, r] = state[1, r] + 0.5 * flux
        state[2, r] = state[2, r] + snow
        state[3, r] = state[3, r] + 0.1 * flux
        state[5, r] = ocean + step * (0.2 * (air[r] - ocean)) - 0.1 * flux * keep[2, r]
        return carry

    def second(r):
        cover, thick, snow, skin, pond, ocean = [state[f, r] for f in range(6)]
        step = 0.5 * wet(r)
        warm = air[r]
        conduction = (ocean - skin) / (softplus(thick) + 0.5 * softplus(snow) + 0.2)
        melting = softplus(skin)
        fraction = sigmoid(cover)
        drained = melting * fraction
        state[0, r] = cover + step * (conduction - melting)
        state[1, r] = thick + step * (0.5 * conduction - drained)
        state[2, r] = snow + step * (gain[r] - 0.5 * melting)
        state[3, r] = skin + step * (warm - skin + 0.1 * conduction)
        state[5, r] = ocean + step * (0.2 * (warm - ocean) - 0.1 * conduction * fraction)
        pond = pond + step * (0.5 * drained)
        state[4, r] = pond
        outflow[1, r + 1] = 0.35 * wet(r) * pond

    column = lax.broadcasted_iota(jnp.int32, (8, 768), 1)
    row = lax.broadcasted_iota(jnp.int32, (8, 768), 0)
    down = {dc: k for k, (dr, dc) in enumerate(DIRECTIONS) if dr == 1}
    up = {dc: k for k, (dr, dc) in enumerate(DIRECTIONS) if dr == -1}
    level = {dc: k for k, (dr, dc) in enumerate(DIRECTIONS) if dr == 0}

    def drain(s, r):
        flows = [outflow[s, r + d] for d in range(3)]
        codes = [code[r + d] for d in range(3)]

        def sent(number, d):
            return jnp.where(codes[d] == number, flows[d], 0.0)

        sums = {}
        for dc in (-1, 0, 1):
            before = pltpu.roll(jnp.where(row == 7, sent(down[dc], 0), sent(down[dc], 1)), 1, 0)
            after = pltpu.roll(jnp.where(row == 0, sent(up[dc], 2), sent(up[dc], 1)), 7, 0)
            sums[dc] = before + after
            if dc:
                sums[dc] = sums[dc] + sent(level[dc], 1)
        right = jnp.where(column == 0, 0.0, pltpu.roll(sums[1], 1, 1))
        left = jnp.where(column == 767, 0.0, pltpu.roll(sums[-1], 767, 1))
        state[4, r] = state[4, r] - flows[1] + wet(r) * (sums[0] + right + left)

    def drain_and_second(r, carry=0):
        drain(0, r)
        second(r)
        return carry

    def drain_last(r, carry=0):
        drain(1, r)
        return carry

    pass_on(0)
    pass_on(1)
    share(0, 1 - c).wait_recv()
    lax.fori_loop(0, 8, melt, 0)
    share(1, 1 - c).wait_recv()
    pool(0)
    pool(7)
    start_edges(outflow.at[0], 1)
    pass_on(2)
    lax.fori_loop(1, 7, pool, 0)
    share(2, 1 - c).wait_recv()
    lax.fori_loop(0, 8, conduct, 0)
    wait_edges(code, 0)
    wait_edges(outflow.at[0], 1)
    drain_and_second(0)
    drain_and_second(7)
    start_edges(outflow.at[1], 2)
    lax.fori_loop(1, 7, drain_and_second, 0)
    lax.fori_loop(1, 7, drain_last, 0)
    wait_edges(outflow.at[1], 2)
    drain_last(0)
    drain_last(7)

    for i in rounds:
        core_copies[i].wait_send()
        remote(pack, pack, plane_send.at[i], plane_recv.at[i], sibling).wait_send()
        depth_copies[i].wait_send()
        remote(pack, pack, gather_send.at[i], gather_recv.at[i], sibling).wait_send()
        share(i, c).wait_send()


def solution(mesh):
    hbm = pl.BlockSpec(memory_space=pltpu.MemorySpace.HBM)
    whole = (6, 8, 8, 768)
    f32, i32 = jnp.float32, jnp.int32
    dma = pltpu.SemaphoreType.DMA

    def shards(members, control, air_temp, flow_codes, ocean_mask):
        rows = (8, 8, 768)
        result = pl.pallas_call(
            kernel,
            out_shape=jax.ShapeDtypeStruct(whole, f32),
            in_specs=[hbm] * 5,
            out_specs=pl.BlockSpec(memory_space=pltpu.VMEM),
            scratch_shapes=[
                pltpu.VMEM(whole, f32), pltpu.VMEM(whole, f32), pltpu.VMEM(whole, f32),
                pltpu.VMEM((3, *rows), f32), pltpu.VMEM((3, PEERS, 8, 384), f32),
                pltpu.VMEM((3, 8, 384), f32), pltpu.VMEM((3, 8, 384), f32),
                pltpu.VMEM((6, 12, 64), f32), pltpu.VMEM(rows, f32), pltpu.VMEM((10, 8, 768), i32),
                pltpu.VMEM(rows, i32), pltpu.VMEM(rows, f32), pltpu.VMEM((3, *rows), f32),
                pltpu.VMEM((SUBSTEPS, 10, 8, 768), f32),
                dma((6,)), *[dma((3,))] * 10, dma((3, 2)), dma((3, 2)),
            ],
            compiler_params=pltpu.CompilerParams(
                collective_id=0, has_side_effects=True, vmem_limit_bytes=VMEM_LIMIT),
            name="recentre_advance",
        )(
            members.reshape(whole), jnp.swapaxes(control, 1, 2), air_temp.reshape(rows),
            flow_codes.reshape(rows), ocean_mask.reshape(rows),
        )
        return result.reshape(1, 6, 64, 768)

    tiles = P("tile", None)
    return jax.shard_map(
        shards, mesh=mesh,
        in_specs=(P("mem", None, "tile", None), P(None, "tile", "mem"), tiles, tiles, tiles),
        out_specs=P("mem", None, "tile", None), check_vma=False)
```

time: 59.9 us -> 46.9 us (0.78)
  Pallas kernels: 53.7 us -> 44.3 us
  local copies, waits for them, and re-layouts: 5.98 us -> 2.39 us
    pallas_call x1, Pallas kernels: 53.7 us -> 44.3 us  [shards(): pl.pallas_call(kernel, out_shape=jax.ShapeDtypeStruct(whole, f32), in_spe...]
    unnamed x10 -> x1, local copies, waits for them, and re-layouts: 5.98 us -> 2.39 us
where the time goes in v2:
time: 46.9 us; the launch traced here: 46.7 us
  Pallas kernels  44.3 us (94%)
  local copies, waits for them, and re-layouts  2.39 us (5%)
    pallas_call x1, Pallas kernels, shards(): pl.pallas_call(kernel, out_shape=jax.ShapeDtypeStruct(whole, f32), in_spe...  44.3 us
    unnamed x1, local copies, waits for them, and re-layouts  2.39 us

profile of v2, /device:TPU:1, one launch (start us, length us, event | category | flops | bytes accessed | tf_op | source)
XLA Modules:
  0.0 46.7 jit_solution(8196248546909280735)
XLA Ops:
  0.0 44.3 %recentre_advance.1 = f32[6,8,8,768]{3,2,1,0:T(8,128)} custom-call(f32[6,8,8,768]{3,2,1,0:T(8,128)} %bitcast.7, f32[6,12,64]{2,1,0:T(8,128)} %bitcast.11, f32[8,8,768]{2,1,0:T(8,128)} %bitcast.8, s32[8,8,768]{2,1,0:T(8,128)} %bitcast.9, s32[8,8,768]{2,1,0:T(8,128)} %bitcast.10), custom_call_target="tpu_custom_call" | custom-call | tf_op jit(solution)/shard_map/recentre_advance/pallas_call | solution.py:309
  44.3 2.4 %copy.7 = f32[1,6,64,768]{3,2,1,0:T(8,128)} copy(f32[1,6,64,768]{3,2,1,0:T(8,128)} %bitcast.6) | data formatting | bytes 2359296

commit v3 on v2

--- a/solution.py
+++ b/solution.py
@@ -7,7 +7,7 @@
 
 MESH = pl.DeviceIdType.MESH
 SUBSTEPS = 2
-VMEM_LIMIT = 60 * 1024 * 1024
+VMEM_LIMIT = 56 * 1024 * 1024
 MEMBERS = 64
 DIRECTIONS = ((0, 1), (1, 1), (1, 0), (1, -1), (0, -1), (-1, -1), (-1, 0), (-1, 1))
 STEPS = sorted(
@@ -36,7 +36,7 @@
 
 def kernel(
     members, control, air_temp, flow_codes, ocean_mask, state,
-    own, raw, shift, core_in, plane_in, depth_out, depth_in, strip, air, code, mask, gain, keep, outflow,
+    own, raw, shift, core_in, plane_in, depth_out, depth_in, strip, air, code, mask, gain, keep, outflow, rim, rim_in,
     local_sem, core_send, core_recv, plane_send, plane_recv, depth_send, depth_recv,
     gather_send, gather_recv, share_send, share_recv, edge_send, edge_recv,
 ):
@@ -95,12 +95,12 @@
     for r in range(8):
         gain[r] = 0.3 * sigmoid(-air[r])
 
-    for edge, missing in ((0, t == 0), (9, t == 7)):
+    for side, edge, missing in ((0, 0, t == 0), (1, 9, t == 7)):
         @pl.when(missing)
         def _():
             code[edge] = jnp.full((8, 768), -1, jnp.int32)
             for s in range(SUBSTEPS):
-                outflow[s, edge] = jnp.zeros((8, 768), jnp.float32)
+                rim_in[s, side] = jnp.zeros((1, 768), jnp.float32)
 
     extra = jnp.where(has_above, 1, 0) + jnp.where(has_below, 1, 0)
     pl.semaphore_wait(barrier, PEERS + 2 + extra)
@@ -109,28 +109,42 @@
         return pltpu.make_async_remote_copy(
             src_ref=src, dst_ref=dst, send_sem=send, recv_sem=recv, device_id=target, device_id_type=MESH)
 
-    def edges(buffer, slot):
-        up = remote(buffer.at[1], buffer.at[9], edge_send.at[slot, 0], edge_recv.at[slot, 0], above)
-        down = remote(buffer.at[8], buffer.at[0], edge_send.at[slot, 1], edge_recv.at[slot, 1], below)
-        return up, down
-
-    def start_edges(buffer, slot):
-        up, down = edges(buffer, slot)
-        pl.when(has_above)(up.start)
-        pl.when(has_below)(down.start)
-
-    def wait_edges(buffer, slot):
-        up, down = edges(buffer, slot)
-
+    def pair(source, goal_, slot):
+        return (
+            remote(source[0], goal_[1], edge_send.at[slot, 0], edge_recv.at[slot, 0], above),
+            remote(source[1], goal_[0], edge_send.at[slot, 1], edge_recv.at[slot, 1], below),
+        )
+
+    def start_pair(upward, downward):
+        pl.when(has_above)(upward.start)
+        pl.when(has_below)(downward.start)
+
+    def wait_pair(upward, downward):
         @pl.when(has_above)
         def _():
-            up.wait_send()
-            down.wait_recv()
+            upward.wait_send()
+            downward.wait_recv()
 
         @pl.when(has_below)
         def _():
-            down.wait_send()
-            up.wait_recv()
+            downward.wait_send()
+            upward.wait_recv()
+
+    code_pair = pair((code.at[1], code.at[8]), (code.at[0], code.at[9]), 0)
+    rim_pairs = [
+        pair((rim.at[s, 0], rim.at[s, 1]), (rim_in.at[s, 0], rim_in.at[s, 1]), 1 + s) for s in range(SUBSTEPS)
+    ]
+
+    def start_rim(s):
+        rim[s, 0] = outflow[s, 0, 0:1]
+        rim[s, 1] = outflow[s, 7, 7:8]
+        start_pair(*rim_pairs[s])
+
+    def wait_rim(s):
+        wait_pair(*rim_pairs[s])
+
+    def wait_edges():
+        wait_pair(*code_pair)
 
     rounds = range(3)
     pack = plane_in.at[0]
@@ -141,7 +155,7 @@
     ]
     for copy in core_copies:
         copy.start()
-    start_edges(code, 0)
+    start_pair(*code_pair)
 
     for i in rounds:
         core_copies[i].wait_recv()
@@ -200,27 +214,22 @@
         drained = keep[0, r]
         pond = field(4, r) + 0.5 * drained
         state[4, r] = pond
-        outflow[0, r + 1] = 0.35 * wet(r) * pond
+        outflow[0, r] = 0.35 * wet(r) * pond
         thick = field(1, r)
         state[1, r] = thick - drained
         keep[0, r] = softplus(thick) + 0.2
         return carry
 
-    def conduct(r, carry=0):
-        ocean, snow = field(5, r), field(2, r)
-        step = 0.5 * wet(r)
-        flux = step * ((ocean - keep[1, r]) / (keep[0, r] + 0.5 * softplus(snow)))
-        state[0, r] = state[0, r] + flux
-        state[1, r] = state[1, r] + 0.5 * flux
-        state[2, r] = state[2, r] + snow
-        state[3, r] = state[3, r] + 0.1 * flux
-        state[5, r] = ocean + step * (0.2 * (air[r] - ocean)) - 0.1 * flux * keep[2, r]
-        return carry
-
-    def second(r):
-        cover, thick, snow, skin, pond, ocean = [state[f, r] for f in range(6)]
+    def finish(r, carry=0):
+        ocean, snow, skin, fraction = field(5, r), field(2, r), keep[1, r], keep[2, r]
         step = 0.5 * wet(r)
         warm = air[r]
+        flux = step * ((ocean - skin) / (keep[0, r] + 0.5 * softplus(snow)))
+        cover = state[0, r] + flux
+        thick = state[1, r] + 0.5 * flux
+        snow = state[2, r] + snow
+        skin = state[3, r] + 0.1 * flux
+        ocean = ocean + step * (0.2 * (warm - ocean)) - 0.1 * flux * fraction
         conduction = (ocean - skin) / (softplus(thick) + 0.5 * softplus(snow) + 0.2)
         melting = softplus(skin)
         fraction = sigmoid(cover)
@@ -230,9 +239,10 @@
         state[2, r] = snow + step * (gain[r] - 0.5 * melting)
         state[3, r] = skin + step * (warm - skin + 0.1 * conduction)
         state[5, r] = ocean + step * (0.2 * (warm - ocean) - 0.1 * conduction * fraction)
-        pond = pond + step * (0.5 * drained)
+        pond = state[4, r] + step * (0.5 * drained)
         state[4, r] = pond
-        outflow[1, r + 1] = 0.35 * wet(r) * pond
+        outflow[1, r] = 0.35 * wet(r) * pond
+        return carry
 
     column = lax.broadcasted_iota(jnp.int32, (8, 768), 1)
     row = lax.broadcasted_iota(jnp.int32, (8, 768), 0)
@@ -241,7 +251,12 @@
     level = {dc: k for k, (dr, dc) in enumerate(DIRECTIONS) if dr == 0}
 
     def drain(s, r):
-        flows = [outflow[s, r + d] for d in range(3)]
+        def flow(d):
+            if isinstance(r, int) and r + d in (-1, 8):
+                return jnp.broadcast_to(rim_in[s, 0 if d < 0 else 1], (8, 768))
+            return outflow[s, r + d]
+
+        flows = [flow(d) for d in (-1, 0, 1)]
         codes = [code[r + d] for d in range(3)]
 
         def sent(number, d):
@@ -258,9 +273,8 @@
         left = jnp.where(column == 767, 0.0, pltpu.roll(sums[-1], 767, 1))
         state[4, r] = state[4, r] - flows[1] + wet(r) * (sums[0] + right + left)
 
-    def drain_and_second(r, carry=0):
+    def drain_first(r, carry=0):
         drain(0, r)
-        second(r)
         return carry
 
     def drain_last(r, carry=0):
@@ -274,21 +288,22 @@
     share(1, 1 - c).wait_recv()
     pool(0)
     pool(7)
-    start_edges(outflow.at[0], 1)
+    start_rim(0)
     pass_on(2)
     lax.fori_loop(1, 7, pool, 0)
+    lax.fori_loop(1, 7, drain_first, 0)
+    wait_edges()
     share(2, 1 - c).wait_recv()
-    lax.fori_loop(0, 8, conduct, 0)
-    wait_edges(code, 0)
-    wait_edges(outflow.at[0], 1)
-    drain_and_second(0)
-    drain_and_second(7)
-    start_edges(outflow.at[1], 2)
-    lax.fori_loop(1, 7, drain_and_second, 0)
+    wait_rim(0)
+    for r in (0, 7):
+        drain(0, r)
+        finish(r)
+    start_rim(1)
+    lax.fori_loop(1, 7, finish, 0)
     lax.fori_loop(1, 7, drain_last, 0)
-    wait_edges(outflow.at[1], 2)
-    drain_last(0)
-    drain_last(7)
+    wait_rim(1)
+    drain(1, 0)
+    drain(1, 7)
 
     for i in rounds:
         core_copies[i].wait_send()
@@ -308,7 +323,7 @@
         rows = (8, 8, 768)
         result = pl.pallas_call(
             kernel,
-            out_shape=jax.ShapeDtypeStruct(whole, f32),
+            out_shape=pltpu.VMEM(whole, f32),
             in_specs=[hbm] * 5,
             out_specs=pl.BlockSpec(memory_space=pltpu.VMEM),
             scratch_shapes=[
@@ -317,7 +332,8 @@
                 pltpu.VMEM((3, 8, 384), f32), pltpu.VMEM((3, 8, 384), f32),
                 pltpu.VMEM((6, 12, 64), f32), pltpu.VMEM(rows, f32), pltpu.VMEM((10, 8, 768), i32),
                 pltpu.VMEM(rows, i32), pltpu.VMEM(rows, f32), pltpu.VMEM((3, *rows), f32),
-                pltpu.VMEM((SUBSTEPS, 10, 8, 768), f32),
+                pltpu.VMEM((SUBSTEPS, 8, 8, 768), f32),
+                pltpu.VMEM((SUBSTEPS, 2, 1, 768), f32), pltpu.VMEM((SUBSTEPS, 2, 1, 768), f32),
                 dma((6,)), *[dma((3,))] * 10, dma((3, 2)), dma((3, 2)),
             ],
             compiler_params=pltpu.CompilerParams(

time: 46.9 us -> 43.5 us (0.928)
  Pallas kernels: 44.3 us -> 42.4 us
  local copies, waits for them, and re-layouts: 2.39 us -> 1.02 us
    pallas_call x1, Pallas kernels: 44.3 us -> 42.4 us  [shards(): pl.pallas_call(kernel, out_shape=pltpu.VMEM(whole, f32), in_specs=[hbm] *...]
    unnamed x1, local copies, waits for them, and re-layouts: 2.39 us -> 1.02 us
where the time goes in v3:
time: 43.5 us; the launch traced here: 43.4 us
  Pallas kernels  42.4 us (97%)
  local copies, waits for them, and re-layouts  1.02 us (2%)
    pallas_call x1, Pallas kernels, shards(): pl.pallas_call(kernel, out_shape=pltpu.VMEM(whole, f32), in_specs=[hbm] *...  42.4 us
    unnamed x1, local copies, waits for them, and re-layouts  1.02 us

profile of v3, /device:TPU:1, one launch (start us, length us, event | category | flops | bytes accessed | tf_op | source)
XLA Modules:
  0.0 43.4 jit_solution(1011303698417975405)
XLA Ops:
  0.0 42.4 %recentre_advance.1 = f32[6,8,8,768]{3,2,1,0:T(8,128)S(1)} custom-call(f32[6,8,8,768]{3,2,1,0:T(8,128)} %bitcast.7, f32[6,12,64]{2,1,0:T(8,128)} %bitcast.11, f32[8,8,768]{2,1,0:T(8,128)} %bitcast.8, s32[8,8,768]{2,1,0:T(8,128)} %bitcast.9, s32[8,8,768]{2,1,0:T(8,128)} %bitcast.10), custom_call_target="tpu_custom_call" | custom-call | tf_op jit(solution)/shard_map/recentre_advance/pallas_call | solution.py:324
  42.4 1.0 %copy.7 = f32[1,6,64,768]{3,2,1,0:T(8,128)} copy(f32[1,6,64,768]{3,2,1,0:T(8,128)S(1)} %bitcast.6) | data formatting | bytes 2359296

commit v4 on v3

--- a/solution.py
+++ b/solution.py
@@ -38,7 +38,7 @@
     members, control, air_temp, flow_codes, ocean_mask, state,
     own, raw, shift, core_in, plane_in, depth_out, depth_in, strip, air, code, mask, gain, keep, outflow, rim, rim_in,
     local_sem, core_send, core_recv, plane_send, plane_recv, depth_send, depth_recv,
-    gather_send, gather_recv, share_send, share_recv, edge_send, edge_recv,
+    gather_send, gather_recv, share_send, share_recv, edge_send, edge_recv, last_recv, outer_send, outer_recv,
 ):
     m, t = lax.axis_index("mem"), lax.axis_index("tile")
     x, y, z, c = m // 16, (m // 4) % 4, (m // 2) % 2, m % 2
@@ -56,6 +56,22 @@
     above, below = (m, jnp.maximum(t - 1, 0)), (m, jnp.minimum(t + 1, 7))
     has_above, has_below = t > 0, t < 7
 
+    def greet(sem, target):
+        pl.semaphore_signal(sem, inc=1, device_id=target, device_id_type=MESH)
+
+    everyone = [far, *(device(a, b, z, c) for a, b in to[:PEERS]), sibling]
+    barrier = pltpu.get_barrier_semaphore()
+    for target in everyone:
+        greet(barrier, target)
+
+    @pl.when(has_above)
+    def _():
+        greet(barrier, above)
+
+    @pl.when(has_below)
+    def _():
+        greet(barrier, below)
+
     loads = [
         pltpu.make_async_copy(s, d, local_sem.at[i])
         for i, (s, d) in enumerate((
@@ -63,20 +79,8 @@
             (flow_codes, code.at[pl.ds(1, 8)]), (members, raw),
         ))
     ]
-    for copy in loads:
+    for copy in loads[:2]:
         copy.start()
-
-    barrier = pltpu.get_barrier_semaphore()
-    for target in [sibling, far] + [device(a, b, z, c) for a, b in to[:PEERS]]:
-        pl.semaphore_signal(barrier, inc=1, device_id=target, device_id_type=MESH)
-
-    @pl.when(has_above)
-    def _():
-        pl.semaphore_signal(barrier, inc=1, device_id=above, device_id_type=MESH)
-
-    @pl.when(has_below)
-    def _():
-        pl.semaphore_signal(barrier, inc=1, device_id=below, device_id_type=MESH)
 
     loads[0].wait()
     loads[1].wait()
@@ -90,18 +94,8 @@
             precision=lax.Precision.HIGHEST, preferred_element_type=jnp.float32)
         for r in range(8):
             own[f, r, :, span] = own[f, r, :, span] + placed[8 * r:8 * r + 8]
-    for i in (2, 3, 4, 5):
-        loads[i].wait()
-    for r in range(8):
-        gain[r] = 0.3 * sigmoid(-air[r])
-
-    for side, edge, missing in ((0, 0, t == 0), (1, 9, t == 7)):
-        @pl.when(missing)
-        def _():
-            code[edge] = jnp.full((8, 768), -1, jnp.int32)
-            for s in range(SUBSTEPS):
-                rim_in[s, side] = jnp.zeros((1, 768), jnp.float32)
-
+    for copy in loads[2:]:
+        copy.start()
     extra = jnp.where(has_above, 1, 0) + jnp.where(has_below, 1, 0)
     pl.semaphore_wait(barrier, PEERS + 2 + extra)
 
@@ -155,7 +149,6 @@
     ]
     for copy in core_copies:
         copy.start()
-    start_pair(*code_pair)
 
     for i in rounds:
         core_copies[i].wait_recv()
@@ -164,6 +157,21 @@
             mine[...] = mine[...] + block(own.at[of_core(i, c)], goal[j])[...]
             if j < PEERS:
                 remote(mine, plane_in.at[i, j], plane_send.at[i], plane_recv.at[i], device(*to[j], z, c)).start()
+
+
+    for i in (2, 3, 4, 5):
+        loads[i].wait()
+    for r in range(8):
+        gain[r] = 0.3 * sigmoid(-air[r])
+
+    for side, edge, missing in ((0, 0, t == 0), (1, 9, t == 7)):
+        @pl.when(missing)
+        def _():
+            code[edge] = jnp.full((8, 768), -1, jnp.int32)
+            for s in range(SUBSTEPS):
+                rim_in[s, side] = jnp.zeros((1, 768), jnp.float32)
+
+    start_pair(*code_pair)
 
     depth_copies = [
         remote(depth_out.at[i], depth_in.at[i], depth_send.at[i], depth_recv.at[i], far) for i in rounds
@@ -181,15 +189,33 @@
         mine = block(shift.at[of_core(i, c)], here)
         mine[...] = (depth_out[i] + depth_in[i]) * (-1.0 / MEMBERS)
         for j in range(PEERS):
-            remote(mine, mine, gather_send.at[i], gather_recv.at[i], device(*to[j], z, c)).start()
+            landed = gather_recv.at[i] if i < 2 else last_recv.at[j]
+            remote(mine, mine, gather_send.at[i], landed, device(*to[j], z, c)).start()
+        if i == 2:
+            remote(mine, mine, share_send.at[i], share_recv.at[i], sibling).start()
 
     def share(i, c):
-        field = shift.at[of_core(i, c)]
-        return remote(field, field, share_send.at[i], share_recv.at[i], sibling)
+        part = shift.at[of_core(i, c)]
+        if i == 1:
+            part = shift.at[of_core(i, c), pl.ds(1, 6)]
+        return remote(part, part, share_send.at[i], share_recv.at[i], sibling)
+
+    def share_outer(k, c):
+        part = shift.at[of_core(1, c), 7 * k]
+        return remote(part, part, outer_send.at[k], outer_recv.at[k], sibling)
 
     def pass_on(i):
         remote(pack, pack, gather_send.at[i], gather_recv.at[i], sibling).wait_recv()
+        if i == 1:
+            share_outer(0, c).start()
+            share_outer(1, c).start()
         share(i, c).start()
+
+    def pass_on_last():
+        for j in range(PEERS):
+            part = block(shift.at[of_core(2, c)], origin[j])
+            remote(part, part, share_send.at[2], last_recv.at[j], sibling).wait_recv()
+            remote(part, part, share_send.at[2], share_recv.at[2], sibling).start()
 
     def field(f, r):
         return raw[f, r] + shift[f, r]
@@ -239,9 +265,17 @@
         state[2, r] = snow + step * (gain[r] - 0.5 * melting)
         state[3, r] = skin + step * (warm - skin + 0.1 * conduction)
         state[5, r] = ocean + step * (0.2 * (warm - ocean) - 0.1 * conduction * fraction)
-        pond = state[4, r] + step * (0.5 * drained)
+        keep[0, r] = step * (0.5 * drained)
+        return carry
+
+    def settle(r):
+        pond = state[4, r] + keep[0, r]
         state[4, r] = pond
         outflow[1, r] = 0.35 * wet(r) * pond
+
+    def finish_and_settle(r, carry=0):
+        finish(r)
+        settle(r)
         return carry
 
     column = lax.broadcasted_iota(jnp.int32, (8, 768), 1)
@@ -282,24 +316,29 @@
         return carry
 
     pass_on(0)
+    share(0, 1 - c).wait_recv()
+    melt(0)
+    melt(7)
     pass_on(1)
-    share(0, 1 - c).wait_recv()
-    lax.fori_loop(0, 8, melt, 0)
+    lax.fori_loop(1, 7, melt, 0)
+    for k in (0, 1):
+        share_outer(k, 1 - c).wait_recv()
+        pool(7 * k)
+    start_rim(0)
     share(1, 1 - c).wait_recv()
-    pool(0)
-    pool(7)
-    start_rim(0)
-    pass_on(2)
+    pass_on_last()
     lax.fori_loop(1, 7, pool, 0)
+    wait_edges()
     lax.fori_loop(1, 7, drain_first, 0)
-    wait_edges()
     share(2, 1 - c).wait_recv()
+    finish(0)
+    finish(7)
     wait_rim(0)
     for r in (0, 7):
         drain(0, r)
-        finish(r)
+        settle(r)
     start_rim(1)
-    lax.fori_loop(1, 7, finish, 0)
+    lax.fori_loop(1, 7, finish_and_settle, 0)
     lax.fori_loop(1, 7, drain_last, 0)
     wait_rim(1)
     drain(1, 0)
@@ -311,6 +350,8 @@
         depth_copies[i].wait_send()
         remote(pack, pack, gather_send.at[i], gather_recv.at[i], sibling).wait_send()
         share(i, c).wait_send()
+    share_outer(0, c).wait_send()
+    share_outer(1, c).wait_send()
 
 
 def solution(mesh):
@@ -335,6 +376,8 @@
                 pltpu.VMEM((SUBSTEPS, 8, 8, 768), f32),
                 pltpu.VMEM((SUBSTEPS, 2, 1, 768), f32), pltpu.VMEM((SUBSTEPS, 2, 1, 768), f32),
                 dma((6,)), *[dma((3,))] * 10, dma((3, 2)), dma((3, 2)),
+                dma((PEERS,)),
+                dma((2,)), dma((2,)),
             ],
             compiler_params=pltpu.CompilerParams(
                 collective_id=0, has_side_effects=True, vmem_limit_bytes=VMEM_LIMIT),

time: 43.5 us -> 43.6 us (level)
  no operation moved by 1% of the time
where the time goes in v4:
time: 43.6 us; the launch traced here: 43.5 us
  Pallas kernels  42.5 us (97%)
  local copies, waits for them, and re-layouts  1.02 us (2%)
    pallas_call x1, Pallas kernels, shards(): pl.pallas_call(kernel, out_shape=pltpu.VMEM(whole, f32), in_specs=[hbm] *...  42.5 us
    unnamed x1, local copies, waits for them, and re-layouts  1.02 us

profile of v4, /device:TPU:1, one launch (start us, length us, event | category | flops | bytes accessed | tf_op | source)
XLA Modules:
  0.0 43.5 jit_solution(15390748856652967938)
XLA Ops:
  0.0 42.5 %recentre_advance.1 = f32[6,8,8,768]{3,2,1,0:T(8,128)S(1)} custom-call(f32[6,8,8,768]{3,2,1,0:T(8,128)} %bitcast.7, f32[6,12,64]{2,1,0:T(8,128)} %bitcast.11, f32[8,8,768]{2,1,0:T(8,128)} %bitcast.8, s32[8,8,768]{2,1,0:T(8,128)} %bitcast.9, s32[8,8,768]{2,1,0:T(8,128)} %bitcast.10), custom_call_target="tpu_custom_call" | custom-call | tf_op jit(solution)/shard_map/recentre_advance/pallas_call | solution.py:365
  42.5 1.0 %copy.7 = f32[1,6,64,768]{3,2,1,0:T(8,128)} copy(f32[1,6,64,768]{3,2,1,0:T(8,128)S(1)} %bitcast.6) | data formatting | bytes 2359296

commit v5 on v4

--- a/solution.py
+++ b/solution.py
@@ -18,7 +18,7 @@
 
 
 def softplus(v):
-    return jnp.maximum(v, 0.0) + jnp.log1p(jnp.exp(-jnp.abs(v)))
+    return jnp.maximum(v, 0.0) + jnp.log(1.0 + jnp.exp(-jnp.abs(v)))
 
 
 def sigmoid(v):
@@ -340,10 +340,6 @@
     start_rim(1)
     lax.fori_loop(1, 7, finish_and_settle, 0)
     lax.fori_loop(1, 7, drain_last, 0)
-    wait_rim(1)
-    drain(1, 0)
-    drain(1, 7)
-
     for i in rounds:
         core_copies[i].wait_send()
         remote(pack, pack, plane_send.at[i], plane_recv.at[i], sibling).wait_send()
@@ -352,6 +348,9 @@
         share(i, c).wait_send()
     share_outer(0, c).wait_send()
     share_outer(1, c).wait_send()
+    wait_rim(1)
+    drain(1, 0)
+    drain(1, 7)
 
 
 def solution(mesh):

time: 43.6 us -> 43.5 us (level)
  no operation moved by 1% of the time
where the time goes in v5:
time: 43.5 us; the launch traced here: 43.4 us
  Pallas kernels  42.4 us (97%)
  local copies, waits for them, and re-layouts  1.02 us (2%)
    pallas_call x1, Pallas kernels, shards(): pl.pallas_call(kernel, out_shape=pltpu.VMEM(whole, f32), in_specs=[hbm] *...  42.4 us
    unnamed x1, local copies, waits for them, and re-layouts  1.02 us

profile of v5, /device:TPU:1, one launch (start us, length us, event | category | flops | bytes accessed | tf_op | source)
XLA Modules:
  0.0 43.4 jit_solution(6042756697184597939)
XLA Ops:
  0.0 42.4 %recentre_advance.1 = f32[6,8,8,768]{3,2,1,0:T(8,128)S(1)} custom-call(f32[6,8,8,768]{3,2,1,0:T(8,128)} %bitcast.7, f32[6,12,64]{2,1,0:T(8,128)} %bitcast.11, f32[8,8,768]{2,1,0:T(8,128)} %bitcast.8, s32[8,8,768]{2,1,0:T(8,128)} %bitcast.9, s32[8,8,768]{2,1,0:T(8,128)} %bitcast.10), custom_call_target="tpu_custom_call" | custom-call | tf_op jit(solution)/shard_map/recentre_advance/pallas_call | solution.py:364
  42.4 1.0 %copy.7 = f32[1,6,64,768]{3,2,1,0:T(8,128)} copy(f32[1,6,64,768]{3,2,1,0:T(8,128)S(1)} %bitcast.6) | data formatting | bytes 2359296

commit v6 on v4

--- a/solution.py
+++ b/solution.py
@@ -38,7 +38,7 @@
     members, control, air_temp, flow_codes, ocean_mask, state,
     own, raw, shift, core_in, plane_in, depth_out, depth_in, strip, air, code, mask, gain, keep, outflow, rim, rim_in,
     local_sem, core_send, core_recv, plane_send, plane_recv, depth_send, depth_recv,
-    gather_send, gather_recv, share_send, share_recv, edge_send, edge_recv, last_recv, outer_send, outer_recv,
+    gather_send, gather_recv, share_send, share_recv, edge_send, edge_recv, plane_ready, depth_near, depth_ready, last_recv, outer_send, outer_recv,
 ):
     m, t = lax.axis_index("mem"), lax.axis_index("tile")
     x, y, z, c = m // 16, (m // 4) % 4, (m // 2) % 2, m % 2
@@ -56,12 +56,20 @@
     above, below = (m, jnp.maximum(t - 1, 0)), (m, jnp.minimum(t + 1, 7))
     has_above, has_below = t > 0, t < 7
 
+    zz = z * 8 + t
+
+    def along(step):
+        place = (zz + step) % 16
+        return (((x * 4 + y) * 2 + place // 8) * 2 + c, place % 8)
+
     def greet(sem, target):
         pl.semaphore_signal(sem, inc=1, device_id=target, device_id_type=MESH)
 
-    everyone = [far, *(device(a, b, z, c) for a, b in to[:PEERS]), sibling]
+    row_peers = [device((x + d) % 4, y, z, c) for d in (2, 1, 3)]
+    column_peers = [device(x, (y + d) % 4, z, c) for d in (2, 1, 3)]
+    near = (along(2), along(14))
     barrier = pltpu.get_barrier_semaphore()
-    for target in everyone:
+    for target in (*near, *row_peers, *column_peers, sibling):
         greet(barrier, target)
 
     @pl.when(has_above)
@@ -97,7 +105,11 @@
     for copy in loads[2:]:
         copy.start()
     extra = jnp.where(has_above, 1, 0) + jnp.where(has_below, 1, 0)
-    pl.semaphore_wait(barrier, PEERS + 2 + extra)
+    pl.semaphore_wait(barrier, 9 + extra)
+    for target in row_peers:
+        greet(plane_ready, target)
+    for target in near:
+        greet(depth_near, target)
 
     def remote(src, dst, send, recv, target):
         return pltpu.make_async_remote_copy(
@@ -150,14 +162,20 @@
     for copy in core_copies:
         copy.start()
 
+    order = [sorted(range(PEERS + 1), key=lambda j: (0 not in STEPS[j] or j == PEERS, j))] + [range(PEERS + 1)] * 2
     for i in rounds:
         core_copies[i].wait_recv()
-        for j in range(PEERS + 1):
+        for j in order[i]:
+            if i == 0 and j == order[0][6]:
+                pl.semaphore_wait(plane_ready, 3)
             mine = block(core_in.at[i], goal[j])
             mine[...] = mine[...] + block(own.at[of_core(i, c)], goal[j])[...]
             if j < PEERS:
                 remote(mine, plane_in.at[i, j], plane_send.at[i], plane_recv.at[i], device(*to[j], z, c)).start()
 
+        if i == 0:
+            pl.semaphore_wait(depth_near, 2)
+            greet(depth_ready, along(12))
 
     for i in (2, 3, 4, 5):
         loads[i].wait()
@@ -182,6 +200,8 @@
         for j in range(PEERS):
             total = total + plane_in[i, j]
         depth_out[i] = total
+        if i == 0:
+            pl.semaphore_wait(depth_ready, 1)
         depth_copies[i].start()
 
     for i in rounds:
@@ -376,7 +396,7 @@
                 pltpu.VMEM((SUBSTEPS, 8, 8, 768), f32),
                 pltpu.VMEM((SUBSTEPS, 2, 1, 768), f32), pltpu.VMEM((SUBSTEPS, 2, 1, 768), f32),
                 dma((6,)), *[dma((3,))] * 10, dma((3, 2)), dma((3, 2)),
-                dma((PEERS,)),
+                *[pltpu.SemaphoreType.REGULAR] * 3, dma((PEERS,)),
                 dma((2,)), dma((2,)),
             ],
             compiler_params=pltpu.CompilerParams(

time: 43.6 us -> 43.6 us (level)
  no operation moved by 1% of the time
where the time goes in v6:
time: 43.6 us; the launch traced here: 43.4 us
  Pallas kernels  42.4 us (97%)
  local copies, waits for them, and re-layouts  1.02 us (2%)
    pallas_call x1, Pallas kernels, shards(): pl.pallas_call(kernel, out_shape=pltpu.VMEM(whole, f32), in_specs=[hbm] *...  42.4 us
    unnamed x1, local copies, waits for them, and re-layouts  1.02 us

profile of v6, /device:TPU:1, one launch (start us, length us, event | category | flops | bytes accessed | tf_op | source)
XLA Modules:
  0.0 43.4 jit_solution(1673493150897198847)
XLA Ops:
  0.0 42.4 %recentre_advance.1 = f32[6,8,8,768]{3,2,1,0:T(8,128)S(1)} custom-call(f32[6,8,8,768]{3,2,1,0:T(8,128)} %bitcast.7, f32[6,12,64]{2,1,0:T(8,128)} %bitcast.11, f32[8,8,768]{2,1,0:T(8,128)} %bitcast.8, s32[8,8,768]{2,1,0:T(8,128)} %bitcast.9, s32[8,8,768]{2,1,0:T(8,128)} %bitcast.10), custom_call_target="tpu_custom_call" | custom-call | tf_op jit(solution)/shard_map/recentre_advance/pallas_call | solution.py:385
  42.4 1.0 %copy.7 = f32[1,6,64,768]{3,2,1,0:T(8,128)} copy(f32[1,6,64,768]{3,2,1,0:T(8,128)S(1)} %bitcast.6) | data formatting | bytes 2359296
